TPU v7x, 32 devices: a whole 2x2x4 slice. The times are simulated.
32 devices in a mesh: row: 4 (over z), col: 8 (over y, x, core).
Axes of the slice: x: 2, y: 2, z: 4, core: 2. Of those that a mesh axis runs over, the one named last changes fastest.
Arguments:
- student: bfloat16 [4096, 2048], P(('row', 'col')), may hold values from -6 to 6
- codes: bfloat16 [4096, 3584], P(('row', 'col')), may hold values from -6 to 6
- scales: bfloat16 [4096, 28], P(('row', 'col')), may hold values from 0.25 to 4
- slot: int32 [4096], P(('row', 'col')), may hold values from 0 to 511, as said below
Outputs:
- loss: float32 [], replicated
- student_grad: float32 [4096, 2048], P(('row', 'col'))
Inputs may be any that keep to these rules, and one draw needn't show every extreme that they name: For the teacher rows held by the devices of one col index, slot lists each of 0 to 511 exactly once.
All inputs are finite; a program needn't handle non-finite values.
Results may differ from a plain program's by a relative error of at most 0.0048.
The roundings to bfloat16 on the way count: a program that leaves them out, or rounds other values in their place, can miss the bound.
Values may be sent and summed in bfloat16 or wider, within the bound.
A program may use at most 128 MiB of HBM per device.

v0:
```python
import jax
import jax.numpy as jnp
from jax import lax
from jax.sharding import PartitionSpec as P


def unit_rows(values):
    inverse_norm = lax.rsqrt(jnp.sum(values * values, axis=1, keepdims=True) + 1e-06)
    return (values * inverse_norm, inverse_norm)


def dequantize(codes, scales):
    rows = codes.shape[0]
    grouped = (
        codes.astype(jnp.float32).reshape(rows, scales.shape[1], -1)
        * scales.astype(jnp.float32)[:, :, None]
    )
    return grouped.reshape(rows, -1)


def on_device(student, codes, scales, slot):
    local_rows = student.shape[0]
    width = student.shape[1]
    unit, inverse_norm = unit_rows(student.astype(jnp.float32))
    student_unit = unit.astype(jnp.bfloat16)
    column_students = lax.all_gather(student_unit, "row", axis=0, tiled=True)
    row_students = lax.all_gather(student_unit, "col", axis=0, tiled=True)
    column_codes, column_scales, column_slots = (
        lax.all_gather(codes, "row", axis=0, tiled=True),
        lax.all_gather(scales, "row", axis=0, tiled=True),
        lax.all_gather(slot, "row", axis=0, tiled=True),
    )
    teacher_server = unit_rows(dequantize(column_codes, column_scales))[0].astype(jnp.bfloat16)
    column_count = column_codes.shape[0]
    inverse_order = (
        jnp.zeros((column_count,), jnp.int32)
        .at[column_slots]
        .set(jnp.arange(column_count, dtype=jnp.int32))
    )
    column_teachers = teacher_server[inverse_order]
    own_teachers = lax.dynamic_slice_in_dim(
        column_teachers, lax.axis_index("row") * local_rows, local_rows, 0
    )
    row_teachers = lax.all_gather(own_teachers, "col", axis=0, tiled=True)
    gram_student = jnp.dot(row_students, column_students.T, preferred_element_type=jnp.float32)
    gram_teacher = jnp.dot(row_teachers, column_teachers.T, preferred_element_type=jnp.float32)
    differ = gram_student - gram_teacher
    total_rows = local_rows * lax.axis_size("row") * lax.axis_size("col")
    loss = lax.psum(jnp.sum(differ * differ), ("row", "col")) * (width / (total_rows * total_rows))
    rounded = differ.astype(jnp.bfloat16)
    grad_unit = lax.psum_scatter(
        1.0 * width * jnp.dot(rounded, column_students, preferred_element_type=jnp.float32),
        "col",
        scatter_dimension=0,
        tiled=True,
    )
    along = jnp.sum(unit * grad_unit, axis=1, keepdims=True)
    student_grad = inverse_norm * (grad_unit - unit * along)
    return (loss, student_grad)


def solution(mesh):
    return jax.shard_map(
        on_device,
        mesh=mesh,
        in_specs=(
            P(("row", "col"), None),
            P(("row", "col"), None),
            P(("row", "col"), None),
            P(("row", "col")),
        ),
        out_specs=(P(), P(("row", "col"), None)),
        check_vma=False,
    )
```

profile of v0, /device:TPU:0, one launch (start us, length us, event | category | flops | bytes accessed | tf_op | source)
XLA Modules:
  0.0 319.3 jit_solution(5274475094761729989)
XLA Ops:
  7.9 1.2 fusion.6
  9.2 2.0 fusion.2
  12.0 13.9 %all_gather.21 = bf16[512,28]{0,1:T(8,128)(2,1)S(1)} all-gather(bf16[128,28]{0,1:T(8,128)(2,1)} %param.6), channel_id=1, replica_groups=mesh['row'=4,'col'=8] {'row'}, dimensions={0}, use_global_device_ids=true | all-gather | bytes 35840 | tf_op jit(solution)/shard_map/all_gather | solution.py:30
  26.0 3.9 %mul.68 = f32[512,28,128]{0,2,1:T(8,128)} broadcast(bf16[512,28]{0,1:T(8,128)(2,1)S(1)} %all_gather.21), dimensions={0,1} | broadcast | bytes 7368704 | tf_op jit(solution)/shard_map/mul | solution.py:15
  29.9 8.4 %copy.8 = f32[512,3584]{1,0:T(8,128)} copy(f32[512,3584]{0,1:T(8,128)} %bitcast.9) | data formatting | bytes 14680064 | tf_op jit(solution)/shard_map/mul | solution.py:15
  38.3 12.3 %all-gather = s32[4,1,128]{2,1,0:T(1,128)S(1)} all-gather(s32[1,1,128]{2,1,0:T(1,128)S(1)} %bitcast.11), channel_id=1, replica_groups=mesh['row'=4,'col'=8] {'row'}, dimensions={0}, use_global_device_ids=true | all-gather | bytes 2560 | tf_op jit(solution)/shard_map/all_gather | solution.py:31
  50.6 2.4 scatter_custom_fusion
  53.1 31.5 %all-gather.10.cloned.1.call-done = bf16[512,3584]{1,0:T(8,128)(2,1)} async-done(((bf16[128,3584]{1,0:T(8,128)(2,1)}), bf16[512,3584]{1,0:T(8,128)(2,1)}) %all-gather.10.cloned.1.call-update) | async-done | bytes 3670032 | tf_op jit(solution)/shard_map/all_gather | solution.py:29
  84.6 5.3 %multiply_reduce_fusion = f32[512]{0:T(512)S(1)} fusion(f32[512,3584]{1,0:T(8,128)} %copy.8, bf16[512,3584]{1,0:T(8,128)(2,1)} %all-gather.10.cloned.1.call-done), kind=kLoop, calls=%fused_computation.3 | loop fusion | flops 7339520 | bytes 11012096 | tf_op jit(solution)/shard_map/reduce_sum | solution.py:8
  89.9 0.9 copy-done
  90.8 1.2 copy-done.1
  92.0 3.4 %multiply_convert_fusion = bf16[512,3584]{1,0:T(8,128)(2,1)} fusion(f32[512,3584]{1,0:T(8,128)S(1)} %copy-done, bf16[512,3584]{1,0:T(8,128)(2,1)S(1)} %copy-done.1, f32[512]{0:T(512)S(1)} %add_rsqrt_fusion), kind=kLoop, calls=%fused_computation.2 | loop fusion | flops 7340032 | bytes 14682112 | tf_op jit(solution)/shard_map/convert_element_type | solution.py:33
  95.3 10.4 %gather_fusion = bf16[512,3584]{1,0:T(8,128)(2,1)} fusion(bf16[512,3584]{1,0:T(8,128)(2,1)} %multiply_convert_fusion, s32[1024]{0:T(1024)S(1)} %pad_clamp_fusion), kind=kCustom, calls=%fused_computation | custom fusion | bytes 7342080 | tf_op jit(solution)/shard_map/gather | solution.py:40
  105.8 2.2 constant_dynamic-slice_fusion
  108.2 22.5 %all-gather.8.cloned.1.call-done = bf16[512,2048]{1,0:T(8,128)(2,1)} async-done(((bf16[128,2048]{1,0:T(8,128)(2,1)}), bf16[512,2048]{1,0:T(8,128)(2,1)}) %all-gather.8.cloned.1.call-update) | async-done | bytes 2097168 | tf_op jit(solution)/shard_map/all_gather | solution.py:26
  130.7 37.4 %all-gather.6.cloned.1.call-done = bf16[1024,2048]{1,0:T(8,128)(2,1)} async-done(((bf16[128,2048]{1,0:T(8,128)(2,1)}), bf16[1024,2048]{1,0:T(8,128)(2,1)}) %all-gather.6.cloned.1.call-update) | async-done | bytes 4194320 | tf_op jit(solution)/shard_map/all_gather | solution.py:27
  168.0 6.6 %fusion.10 = f32[1024,512]{1,0:T(8,128)} fusion(bf16[1024,2048]{1,0:T(8,128)(2,1)} %all-gather.6.cloned.1.call-done, bf16[512,2048]{1,0:T(8,128)(2,1)} %all-gather.8.cloned.1.call-done), kind=kOutput, calls=%fused_computation.26 | convolution fusion | flops 2147483648 | bytes 8388608 | tf_op jit(solution)/shard_map/dot_general | solution.py:45
  174.6 45.7 %all-gather.12.cloned.1.call-done = bf16[1024,3584]{1,0:T(8,128)(2,1)} async-done(((bf16[128,3584]{1,0:T(8,128)(2,1)}), bf16[1024,3584]{1,0:T(8,128)(2,1)}) %all-gather.12.cloned.1.call-update) | async-done | bytes 7340048 | tf_op jit(solution)/shard_map/all_gather | solution.py:44
  220.3 9.6 %multiply_reduce_fusion.1 = (f32[]{:T(128)}, bf16[1024,512]{1,0:T(8,128)(2,1)S(1)}) fusion(f32[1024,512]{1,0:T(8,128)} %fusion.10, bf16[1024,3584]{1,0:T(8,128)(2,1)} %all-gather.12.cloned.1.call-done, bf16[512,3584]{1,0:T(8,128)(2,1)} %gather_fusion), kind=kOutput, calls=%fused_computation.6 | convolution fusion | flops 3760193536 | bytes 14155780 | tf_op jit(solution)/shard_map/dot_general | solution.py:46
  230.0 5.6 %convolution_multiply_fusion = f32[1024,2048]{1,0:T(8,128)} fusion(bf16[512,2048]{1,0:T(8,128)(2,1)S(1)} %copy-done.4, bf16[1024,512]{1,0:T(8,128)(2,1)S(1)} %get-tuple-element.3), kind=kOutput, calls=%fused_computation.5 | convolution fusion | flops 2149580800 | bytes 11534336 | tf_op jit(solution)/shard_map/dot_general | solution.py:52
  235.6 39.9 %psum.7 = f32[]{:T(128)} all-reduce(f32[]{:T(128)} %get-tuple-element.2), channel_id=1, replica_groups=mesh['row'=4,'col'=8] {'row','col'}, use_global_device_ids=true, to_apply=%region_4.0 | all-reduce | flops 1 | bytes 8 | tf_op jit(solution)/shard_map/psum | solution.py:49
  276.1 31.5 %reduce-scatter.2.cloned.1.call-done = f32[128,2048]{1,0:T(8,128)} async-done(((f32[1024,2048]{1,0:T(8,128)}), f32[128,2048]{1,0:T(8,128)}) %reduce-scatter.2.cloned.1.call-update) | async-done | bytes 1048592 | tf_op jit(solution)/shard_map/reduce_scatter | solution.py:51
  307.6 1.5 fusion.3
  309.1 2.5 fusion.5
  (24 shorter events, 1.8 us)
Async XLA Ops:
  7.2 77.4 %all-gather.10.cloned.1.call-start = ((), (), s32[]{:S(2)}) async-start(), calls=%async_computation.3 | async-start | bytes 4587520 | tf_op jit(solution)/shard_map/all_gather | solution.py:29
  7.9 122.8 %all-gather.8.cloned.1.call-start = ((), (), s32[]{:S(2)}) async-start(), calls=%async_computation.2 | async-start | bytes 2621440 | tf_op jit(solution)/shard_map/all_gather | solution.py:26
  11.2 156.8 %all-gather.6.cloned.1.call-start = ((), (), s32[]{:S(2)}) async-start(), calls=%async_computation.1 | async-start | bytes 4718592 | tf_op jit(solution)/shard_map/all_gather | solution.py:27
  12.0 208.4 %all-gather.12.cloned.1.call-start = ((), (), s32[]{:S(2)}) async-start(), calls=%async_computation.4 | async-start | bytes 8257536 | tf_op jit(solution)/shard_map/all_gather | solution.py:44
  29.9 8.4 %copy-start.3 = (s32[128]{0:T(128)S(1)}, s32[128]{0:T(128)}, u32[]{:S(2)}) copy-start(s32[128]{0:T(128)} %param.7) | copy-start | bytes 1540
  84.6 6.2 %copy-start = (f32[512,3584]{1,0:T(8,128)S(1)}, f32[512,3584]{1,0:T(8,128)}, u32[]{:S(2)}) copy-start(f32[512,3584]{1,0:T(8,128)} %copy.8) | copy-start | bytes 22020100
  84.6 7.4 %copy-start.1 = (bf16[512,3584]{1,0:T(8,128)(2,1)S(1)}, bf16[512,3584]{1,0:T(8,128)(2,1)}, u32[]{:S(2)}) copy-start(bf16[512,3584]{1,0:T(8,128)(2,1)} %all-gather.10.cloned.1.call-done) | copy-start | bytes 11010052
  108.0 199.7 %reduce-scatter.2.cloned.1.call-start = ((), (), s32[]{:S(2)}) async-start(), calls=%async_computation.5 | async-start | bytes 9437184 | tf_op jit(solution)/shard_map/reduce_scatter | solution.py:51
  174.6 55.4 %copy-start.4 = (bf16[512,2048]{1,0:T(8,128)(2,1)S(1)}, bf16[512,2048]{1,0:T(8,128)(2,1)}, u32[]{:S(2)}) copy-start(bf16[512,2048]{1,0:T(8,128)(2,1)} %all-gather.8.cloned.1.call-done) | copy-start | bytes 6291460
  235.5 72.1 %copy-start.2 = (bf16[128,2048]{1,0:T(8,128)(2,1)S(1)}, bf16[128,2048]{1,0:T(8,128)(2,1)}, u32[]{:S(2)}) copy-start(bf16[128,2048]{1,0:T(8,128)(2,1)} %param.4) | copy-start | bytes 1572868
Sparse Core Ops, SparseCore 0:
  9.6 74.9 all-gather.9
  86.1 44.4 all-gather.7
  132.6 35.4 all-gather.5
  170.3 49.9 all-gather.11
  235.7 71.8 reduce-scatter.1
where the time goes:
time: 320 us; the launch traced here: 319 us
  waiting for transfers between devices  170 us (53%)
  blocking collectives  66.1 us (21%)
  local copies, waits for them, and re-layouts  29.4 us (9%)
  matrix products  21.8 us (7%)
  other arithmetic  16 us (5%)
  between operations  15.6 us (5%)
    all_gather x1, waiting for transfers between devices, on_device(): row_teachers = lax.all_gather(own_teachers, 'col', axis=0, tiled=True)  45.7 us
    psum x1, blocking collectives, on_device(): lax.psum(jnp.sum(differ * differ), ('row', 'col'))  39.9 us
    all_gather x1, waiting for transfers between devices, on_device(): row_students = lax.all_gather(student_unit, 'col', axis=0, tiled=True)  37.4 us
    all_gather x1, waiting for transfers between devices, on_device(): lax.all_gather(codes, 'row', axis=0, tiled=True)  31.5 us
    reduce_scatter x1, waiting for transfers between devices, on_device(): lax.psum_scatter(1.0 * width * jnp.dot(rounded, column_students, preferre...  31.5 us
    all_gather x1, waiting for transfers between devices, on_device(): column_students = lax.all_gather(student_unit, 'row', axis=0, tiled=True)  22.5 us
    all_gather x1, blocking collectives, on_device(): lax.all_gather(scales, 'row', axis=0, tiled=True)  13.9 us
    mul x2, local copies, waits for them, and re-layouts, dequantize(): codes.astype(jnp.float32).reshape(rows, scales.shape[1], -1)  12.3 us
  transfers between devices with their start and end apart: 5, of which 5 were waited for; matrix products, arithmetic and copies ran while one was open for 14% of the time, Pallas kernels for 0%

commit v1 on v0

v1 whole, which is shorter than its diff:
```python
import functools

import jax
import jax.numpy as jnp
from jax import lax
from jax.experimental import pallas as pl
from jax.experimental.pallas import tpu as pltpu
from jax.sharding import PartitionSpec as P

MESH = pl.DeviceIdType.MESH
F32 = jnp.float32
BF16 = jnp.bfloat16


def flip(index, bit):
    return index + bit * (1 - 2 * ((index // bit) % 2))


def flip_all(index, mask):
    bit = 1
    while bit <= mask:
        if mask & bit:
            index = flip(index, bit)
        bit *= 2
    return index


def kernel(
    rows_n, cols_n, total_rows, student, codes, scales, slot, loss_out, grad_out,
    s_row, s_col, t_raw, t_col, t_row, places, slots, core_got, got, total,
    loss_z, loss_put, loss_got, loss_sum, send, recv,
):
    r = student.shape[0]
    ds = student.shape[1]
    dt = codes.shape[1]
    group = dt // scales.shape[1]
    a = lax.axis_index("row")
    c = lax.axis_index("col")
    chips = cols_n // 2
    bits = []
    bit = cols_n // 2
    while bit > 1:
        bits.append(bit)
        bit //= 2
    orders = (tuple(bits), tuple(reversed(bits)))
    core = c % 2
    chip = c // 2
    counter = [0]

    def take(count=1):
        counter[0] += count
        return counter[0] - count

    def copy_to(src, dst, index, device):
        return pltpu.make_async_remote_copy(
            src_ref=src, dst_ref=dst, send_sem=send.at[index], recv_sem=recv.at[index],
            device_id=device, device_id_type=MESH,
        )

    def block(index, size=r):
        return pl.ds(pl.multiple_of(index * size, size), size)

    barrier = pltpu.get_barrier_semaphore()
    for k in range(1, rows_n):
        pl.semaphore_signal(barrier, inc=1, device_id=((a + k) % rows_n, c), device_id_type=MESH)
    for bit in bits + [1]:
        pl.semaphore_signal(barrier, inc=1, device_id=(a, flip(c, bit)), device_id_type=MESH)

    squares = jnp.zeros((r, group), F32)
    for g in range(dt // group):
        part = codes[:, g * group:(g + 1) * group].astype(F32) * scales[:, g:g + 1].astype(F32)
        squares = squares + part * part
    inverse = lax.rsqrt(jnp.sum(squares, axis=1, keepdims=True) + 1e-06)
    for g in range(dt // group):
        part = codes[:, g * group:(g + 1) * group].astype(F32) * scales[:, g:g + 1].astype(F32)
        t_raw[block(a), g * group:(g + 1) * group] = (part * inverse).astype(BF16)
    slots[a] = jnp.broadcast_to(slot[...], slots.shape[1:])

    pl.semaphore_wait(barrier, rows_n - 1 + len(bits) + 1)

    def line(refs):
        base = take(len(refs) * 2 * (rows_n - 1))

        def each(step, up, act):
            for n, (ref, view) in enumerate(refs):
                index = base + (n * 2 + up) * (rows_n - 1) + step
                act(ref, view, index)

        def start(step):
            for up in (1, 0):
                held = a - step if up else a + step
                ok = (held >= 0) & (a < rows_n - 1) if up else (held < rows_n) & (a > 0)
                to = (a + 1 if up else a - 1, c)

                @pl.when(ok)
                def _():
                    each(step, up, lambda ref, view, index: copy_to(
                        view(ref, held), view(ref, held), index, to).start())

        def wait_recv(step):
            for up in (1, 0):
                held = a - 1 - step if up else a + 1 + step
                ok = held >= 0 if up else held < rows_n

                @pl.when(ok)
                def _():
                    each(step, up, lambda ref, view, index: copy_to(
                        view(ref, held), view(ref, held), index, (a, c)).wait_recv())

        def wait_send():
            for step in range(rows_n - 1):
                for up in (1, 0):
                    held = a - step if up else a + step
                    ok = (held >= 0) & (a < rows_n - 1) if up else (held < rows_n) & (a > 0)

                    @pl.when(ok)
                    def _():
                        each(step, up, lambda ref, view, index: copy_to(
                            view(ref, held), view(ref, held), index, (a, c)).wait_send())

        return start, wait_recv, wait_send

    def plane(ref, width):
        half = width // 2
        started = []
        steps = len(bits)
        pending = {}

        def start(step):
            todo = []
            for h in (0, 1):
                order = orders[h]
                masks = [0]
                for bit in order[:step]:
                    masks = masks + [mask + bit for mask in masks]
                for mask in masks:
                    index = take()
                    view = ref.at[block(flip_all(c, mask)), h * half:(h + 1) * half]
                    copy = copy_to(view, view, index, (a, flip(c, order[step])))
                    copy.start()
                    started.append(copy)
                    todo.append(copy)
            pending[step] = todo

        def start_core():
            todo = []
            for mask in range(0, cols_n, 2):
                index = take()
                view = ref.at[block(flip_all(c, mask)), 0:width]
                copy = copy_to(view, view, index, (a, flip(c, 1)))
                copy.start()
                started.append(copy)
                todo.append(copy)
            pending[steps] = todo

        def wait_recv(step):
            for copy in pending[step]:
                copy.wait_recv()

        def wait_send():
            for copy in started:
                copy.wait_send()

        return start, start_core, wait_recv, wait_send

    whole = lambda ref, held: ref.at[block(held)]
    page = lambda ref, held: ref.at[held]
    t_start, t_recv, t_sent = line([(t_raw, whole), (slots, page)])
    t_start(0)

    values = student[...].astype(F32)
    inverse_norm = lax.rsqrt(jnp.sum(values * values, axis=1, keepdims=True) + 1e-06)
    unit = (values * inverse_norm).astype(BF16)
    s_row[block(c)] = unit
    s_col[block(a)] = unit

    steps = len(bits)
    p_start, p_core, p_recv, p_sent = plane(s_row, ds)
    p_start(0)
    p_recv(0)
    for step in range(1, steps):
        p_start(step)
        p_recv(step)
    p_core()
    for step in range(rows_n - 1):
        t_recv(step)
        if step + 1 < rows_n - 1:
            t_start(step + 1)

    s_start, s_recv, s_sent = line([(s_col, whole)])
    s_start(0)

    column = rows_n * r
    for b in range(rows_n):
        at = lax.broadcasted_iota(jnp.int32, (column, r), 0)
        places[:, b * r:(b + 1) * r] = (at == slots[b][0:1, :]).astype(F32).astype(BF16)
    piece = 512

    def own(n, carry):
        cut = block(n, piece)
        t_row[block(c), cut] = jnp.dot(
            places[block(a), :], t_raw[:, cut], preferred_element_type=F32).astype(BF16)
        return carry

    lax.fori_loop(0, dt // piece, own, 0)
    q_start, q_core, q_recv, q_sent = plane(t_row, dt)
    q_start(0)

    def every(n, carry):
        cut = block(n, piece)
        t_col[:, cut] = jnp.dot(places[...], t_raw[:, cut], preferred_element_type=F32).astype(BF16)
        return carry

    lax.fori_loop(0, dt // piece, every, 0)
    q_recv(0)
    for step in range(1, steps):
        q_start(step)
        if step <= rows_n - 2:
            s_recv(step - 1)
            s_start(step)
        q_recv(step)
    q_core()
    for step in range(min(steps, rows_n - 1) - 1, rows_n - 1):
        s_recv(step)
        if step + 1 < rows_n - 1:
            s_start(step + 1)
    p_recv(steps)
    q_recv(steps)
    q_sent()

    loss_sum[...] = jnp.zeros_like(loss_sum)
    core_base = take(chips)
    contract = (((1,), (1,)), ((), ()))

    def core_copy(i, there):
        return copy_to(
            t_row.at[block(there * 2 + 1 - core), 0:ds], core_got.at[i], core_base + i, (a, flip(c, 1)))

    def tile(i, carry):
        there = (chip + 1 + i) % chips
        pair = block(there, 2 * r)
        differ = lax.dot_general(s_row[pair, :], s_col[...], contract, preferred_element_type=F32)
        differ = differ - lax.dot_general(t_row[pair, :], t_col[...], contract, preferred_element_type=F32)
        loss_sum[...] += jnp.sum(differ * differ, axis=0, keepdims=True)
        low = differ.astype(BF16)
        for n in range(ds // piece):
            t_row[pair, n * piece:(n + 1) * piece] = jnp.dot(
                low, s_col[:, n * piece:(n + 1) * piece], preferred_element_type=F32).astype(BF16)
        core_copy(i, there).start()
        return carry

    lax.fori_loop(0, chips, tile, 0)

    loss_z[a] = jnp.broadcast_to(jnp.sum(loss_sum[...], axis=1, keepdims=True), loss_z.shape[1:])
    loss_copies = []
    for k in range(1, rows_n):
        copy = copy_to(loss_z.at[a], loss_z.at[a], take(), ((a + k) % rows_n, c))
        copy.start()
        loss_copies.append(copy)

    def join(i, carry):
        there = (chip + 1 + i) % chips
        core_copy(i, there).wait_recv()
        mine = block(there * 2 + core)
        t_row[mine, 0:ds] = (t_row[mine, 0:ds].astype(F32) + core_got[i].astype(F32)).astype(BF16)
        return carry

    lax.fori_loop(0, chips - 1, join, 0)
    core_copy(chips - 1, chip).wait_recv()
    total[...] = t_row[block(c), 0:ds].astype(F32) + core_got[chips - 1].astype(F32)

    half = ds // 2
    left = [list(range(0, cols_n, 2)) for _ in (0, 1)]
    sent = []
    got_at = 0
    for k, copy in enumerate(loss_copies):
        copy.wait_recv()
    loss_now = loss_z[0]
    for b in range(1, rows_n):
        loss_now = loss_now + loss_z[b]
    loss_bits = bits + [1]
    for step in range(steps):
        todo = []
        loss_put[step] = loss_now
        loss_copy = copy_to(loss_put.at[step], loss_got.at[step], take(), (a, flip(c, loss_bits[step])))
        loss_copy.start()
        for h in (0, 1):
            bit = tuple(reversed(orders[h]))[step]
            keep = [mask for mask in left[h] if not mask & bit]
            for mask in keep:
                away = t_row.at[block(flip_all(c, mask + bit)), h * half:(h + 1) * half]
                copy = copy_to(away, got.at[got_at], take(), (a, flip(c, bit)))
                copy.start()
                todo.append((h, mask, copy, got_at))
                got_at += 1
            left[h] = keep
        loss_copy.wait_recv()
        loss_now = loss_now + loss_got[step]
        sent.append(loss_copy)
        for h, mask, copy, index in todo:
            copy.wait_recv()
            sent.append(copy)
            span = slice(h * half, (h + 1) * half)
            if mask == 0:
                total[:, span] += got[index].astype(F32)
            else:
                mine = block(flip_all(c, mask))
                t_row[mine, span] = (t_row[mine, span].astype(F32) + got[index].astype(F32)).astype(BF16)
    loss_put[steps] = loss_now
    copy = copy_to(loss_put.at[steps], loss_got.at[steps], take(), (a, flip(c, 1)))
    copy.start()
    sent.append(copy)

    grad = total[...] * float(ds)
    values = student[...].astype(F32)
    inverse_norm = lax.rsqrt(jnp.sum(values * values, axis=1, keepdims=True) + 1e-06)
    unit = values * inverse_norm
    along = jnp.sum(unit * grad, axis=1, keepdims=True)
    grad_out[...] = inverse_norm * (grad - unit * along)

    copy.wait_recv()
    loss_out[...] = (loss_now + loss_got[steps]) * (ds / (total_rows * total_rows))

    for copy in sent + loss_copies:
        copy.wait_send()
    for i in range(chips):
        core_copy(i, (chip + 1 + i) % chips).wait_send()
    t_sent()
    s_sent()
    p_sent()


def on_device(rows_n, cols_n, student, codes, scales, slot):
    r, ds = student.shape
    dt = codes.shape[1]
    total_rows = r * rows_n * cols_n
    chips = cols_n // 2
    steps = chips.bit_length() - 1
    count = 6 * (rows_n - 1) + 2 * (2 * (chips - 1) + chips)
    count += chips + (rows_n - 1) + 2 * (chips - 1) + steps + 1
    vmem = pl.BlockSpec(memory_space=pltpu.VMEM)
    loss, grad = pl.pallas_call(
        functools.partial(kernel, rows_n, cols_n, total_rows),
        out_shape=(jax.ShapeDtypeStruct((8, 128), F32), jax.ShapeDtypeStruct((r, ds), F32)),
        in_specs=[vmem] * 4,
        out_specs=(vmem, vmem),
        scratch_shapes=[
            pltpu.VMEM((cols_n * r, ds), BF16),
            pltpu.VMEM((rows_n * r, ds), BF16),
            pltpu.VMEM((rows_n * r, dt), BF16),
            pltpu.VMEM((rows_n * r, dt), BF16),
            pltpu.VMEM((cols_n * r, dt), BF16),
            pltpu.VMEM((rows_n * r, rows_n * r), BF16),
            pltpu.VMEM((rows_n, 8, r), jnp.int32),
            pltpu.VMEM((chips, r, ds), BF16),
            pltpu.VMEM((2 * (chips - 1), r, ds // 2), BF16),
            pltpu.VMEM((r, ds), F32),
            pltpu.VMEM((rows_n, 8, 128), F32),
            pltpu.VMEM((steps + 1, 8, 128), F32),
            pltpu.VMEM((steps + 1, 8, 128), F32),
            pltpu.VMEM((1, rows_n * r), F32),
            pltpu.SemaphoreType.DMA((count,)),
            pltpu.SemaphoreType.DMA((count,)),
        ],
        compiler_params=pltpu.CompilerParams(
            collective_id=0, has_side_effects=True, vmem_limit_bytes=62 * 1024 * 1024
        ),
    )(student, codes, scales, slot.reshape(1, r))
    return loss[0, 0], grad


def solution(mesh):
    rows_n, cols_n = mesh.shape["row"], mesh.shape["col"]
    return jax.shard_map(
        functools.partial(on_device, rows_n, cols_n),
        mesh=mesh,
        in_specs=(
            P(("row", "col"), None),
            P(("row", "col"), None),
            P(("row", "col"), None),
            P(("row", "col")),
        ),
        out_specs=(P(), P(("row", "col"), None)),
        check_vma=False,
    )
```

time: 320 us -> 147 us (0.46)
  waiting for transfers between devices: 170 us -> 0 us
  Pallas kernels: 0 us -> 141 us
  blocking collectives: 66.1 us -> 0 us
  local copies, waits for them, and re-layouts: 29.4 us -> 4.9 us
  matrix products: 21.8 us -> 0 us
  other arithmetic: 16 us -> 0 us
  between operations: 15.6 us -> 0.64 us
    pallas_call x0 -> x1, Pallas kernels: none -> 141 us  [on_device(): pl.pallas_call(functools.partial(kernel, rows_n, cols_n, total_rows), out...]
    all_gather x4 -> x0, waiting for transfers between devices: 137 us -> none  [the longest x1 45.7 us: on_device(): row_teachers = lax.all_gather(own_teachers, 'col', axis=0, tiled=True)]
    psum x1 -> x0, blocking collectives: 39.9 us -> none  [on_device(): lax.psum(jnp.sum(differ * differ), ('row', 'col'))]
    reduce_scatter x1 -> x0, waiting for transfers between devices: 31.5 us -> none  [on_device(): lax.psum_scatter(1.0 * width * jnp.dot(rounded, column_students, preferre...]
    all_gather x2 -> x0, blocking collectives: 26.2 us -> none  [the longest x1 13.9 us: on_device(): lax.all_gather(scales, 'row', axis=0, tiled=True)]
    dot_general x3 -> x0, matrix products: 21.8 us -> none  [the longest x1 9.65 us: on_device(): jnp.dot(row_teachers, column_teachers.T, preferred_element_type=jnp.float32)]
    mul x2 -> x0, local copies, waits for them, and re-layouts: 12.3 us -> none  [dequantize(): codes.astype(jnp.float32).reshape(rows, scales.shape[1], -1)]
    gather x1 -> x0, local copies, waits for them, and re-layouts: 10.4 us -> none  [on_device(): column_teachers = teacher_server[inverse_order]]
  transfers between devices with their start and end apart: 5 -> 0, of which waited for: 5 -> 0; matrix products, arithmetic and copies ran while one was open for 14% -> 0% of each run, Pallas kernels for 0% -> 0%
where the time goes in v1:
time: 147 us
  Pallas kernels  141 us (96%)
  local copies, waits for them, and re-layouts  4.9 us (3%)
    pallas_call x1, Pallas kernels, on_device(): pl.pallas_call(functools.partial(kernel, rows_n, cols_n, total_rows), out...  141 us
    unnamed x2, local copies, waits for them, and re-layouts  3.71 us

profile of v1, /device:TPU:0, one launch (start us, length us, event | category | flops | bytes accessed | tf_op | source)
XLA Modules:
  0.0 146.6 jit_solution(3077042662306015053)
XLA Ops:
  0.6 1.4 copy.6.scales
  2.0 141.1 %shard_map.59 = (f32[8,128]{1,0:T(8,128)}, f32[128,2048]{1,0:T(8,128)}) custom-call(bf16[128,2048]{1,0:T(8,128)(2,1)} %student.1, bf16[128,3584]{1,0:T(8,128)(2,1)} %codes.1, bf16[128,28]{1,0:T(8,128)(2,1)} %copy.6.scales, s32[1,128]{1,0:T(1,128)} %bitcast.2), custom_call_target="tpu_custom_call" | custom-call | tf_op jit(solution)/shard_map/pallas_call | solution.py:342
  143.1 1.2 slice.3
  144.3 2.3 %copy.8 = f32[128,2048]{1,0:T(8,128)} copy(f32[128,2048]{1,0:T(8,128)} %get-tuple-element.9) | data formatting | bytes 2097152

commit v2 on v1

v2 whole, which is shorter than its diff:
```python
import functools

import jax
import jax.numpy as jnp
from jax import lax
from jax.experimental import pallas as pl
from jax.experimental.pallas import tpu as pltpu
from jax.sharding import PartitionSpec as P

MESH = pl.DeviceIdType.MESH
F32 = jnp.float32
BF16 = jnp.bfloat16


def flip(index, bit):
    return index + bit * (1 - 2 * ((index // bit) % 2))


def flip_all(index, mask):
    bit = 1
    while bit <= mask:
        if mask & bit:
            index = flip(index, bit)
        bit *= 2
    return index


def kernel(
    rows_n, cols_n, total_rows, student, codes, scales, slot, loss_out, grad_out,
    s_row, s_col, t_raw, t_col, t_row, places, slots, differ, got, total,
    loss_z, loss_put, loss_got, loss_sum, send, recv,
):
    r = student.shape[0]
    ds = student.shape[1]
    dt = codes.shape[1]
    group = dt // scales.shape[1]
    a = lax.axis_index("row")
    c = lax.axis_index("col")
    chips = cols_n // 2
    bits = []
    bit = cols_n // 2
    while bit > 1:
        bits.append(bit)
        bit //= 2
    orders = (tuple(bits), tuple(reversed(bits)))
    core = c % 2
    chip = c // 2
    counter = [0]

    def take(count=1):
        counter[0] += count
        return counter[0] - count

    def copy_to(src, dst, index, device):
        return pltpu.make_async_remote_copy(
            src_ref=src, dst_ref=dst, send_sem=send.at[index], recv_sem=recv.at[index],
            device_id=device, device_id_type=MESH,
        )

    def block(index, size=r):
        return pl.ds(pl.multiple_of(index * size, size), size)

    barrier = pltpu.get_barrier_semaphore()
    for k in range(1, rows_n):
        pl.semaphore_signal(barrier, inc=1, device_id=((a + k) % rows_n, c), device_id_type=MESH)
    for bit in bits + [1]:
        pl.semaphore_signal(barrier, inc=1, device_id=(a, flip(c, bit)), device_id_type=MESH)

    slots[a] = jnp.broadcast_to(slot[...], slots.shape[1:])
    cut_rows = r // 2

    def teacher(part):
        rows = slice(part * cut_rows, (part + 1) * cut_rows)
        squares = jnp.zeros((cut_rows, group), F32)
        for g in range(dt // group):
            value = codes[rows, g * group:(g + 1) * group].astype(F32) * scales[rows, g:g + 1].astype(F32)
            squares = squares + value * value
        inverse = lax.rsqrt(jnp.sum(squares, axis=1, keepdims=True) + 1e-06)
        to = block(2 * a + part, cut_rows)
        for g in range(dt // group):
            value = codes[rows, g * group:(g + 1) * group].astype(F32) * scales[rows, g:g + 1].astype(F32)
            t_raw[to, g * group:(g + 1) * group] = (value * inverse).astype(BF16)

    def line(refs):
        base = take(len(refs) * 2 * (rows_n - 1))

        def each(step, up, parts, act):
            for n, (ref, view) in enumerate(refs):
                if n in parts:
                    act(ref, view, base + (n * 2 + up) * (rows_n - 1) + step)

        every_part = tuple(range(len(refs)))

        def start(step, parts=every_part):
            for up in (1, 0):
                held = a - step if up else a + step
                ok = (held >= 0) & (a < rows_n - 1) if up else (held < rows_n) & (a > 0)
                to = (a + 1 if up else a - 1, c)

                @pl.when(ok)
                def _():
                    each(step, up, parts, lambda ref, view, index: copy_to(
                        view(ref, held), view(ref, held), index, to).start())

        def wait_recv(step, parts=every_part):
            for up in (1, 0):
                held = a - 1 - step if up else a + 1 + step
                ok = held >= 0 if up else held < rows_n

                @pl.when(ok)
                def _():
                    each(step, up, parts, lambda ref, view, index: copy_to(
                        view(ref, held), view(ref, held), index, (a, c)).wait_recv())

        def wait_send():
            for step in range(rows_n - 1):
                for up in (1, 0):
                    held = a - step if up else a + step
                    ok = (held >= 0) & (a < rows_n - 1) if up else (held < rows_n) & (a > 0)

                    @pl.when(ok)
                    def _():
                        each(step, up, every_part, lambda ref, view, index: copy_to(
                            view(ref, held), view(ref, held), index, (a, c)).wait_send())

        return start, wait_recv, wait_send

    def plane(ref, width):
        half = width // 2
        started = []
        hops, cores = {}, {}

        def hop(h, step, mask):
            view = ref.at[block(flip_all(c, mask)), h * half:(h + 1) * half]
            hops[h, step, mask] = copy_to(view, view, take(), (a, flip(c, orders[h][step])))
            hops[h, step, mask].start()
            started.append(hops[h, step, mask])

        def to_core(h, mask):
            view = ref.at[block(flip_all(c, mask)), h * half:(h + 1) * half]
            cores[h, mask] = copy_to(view, view, take(), (a, flip(c, 1)))
            cores[h, mask].start()
            started.append(cores[h, mask])

        def start():
            for step in range(len(bits)):
                for h in (0, 1):
                    hop(h, step, 0)
            for h in (0, 1):
                to_core(h, 0)

        def pass_on(step):
            for h in (0, 1):
                masks = [0]
                for bit in orders[h][:step]:
                    masks = masks + [mask + bit for mask in masks]
                for mask in masks:
                    hops[h, step, mask].wait_recv()
                    held = mask + orders[h][step]
                    for later in range(step + 1, len(bits)):
                        hop(h, later, held)
                    to_core(h, held)

        def wait_core():
            for copy in cores.values():
                copy.wait_recv()

        def wait_send():
            for copy in started:
                copy.wait_send()

        return start, pass_on, wait_core, wait_send

    whole = lambda ref, held: ref.at[block(held)]
    page = lambda ref, held: ref.at[held]
    first = lambda ref, held: ref.at[block(2 * held, cut_rows)]
    second = lambda ref, held: ref.at[block(2 * held + 1, cut_rows)]
    t_start, t_recv, t_sent = line([(t_raw, first), (t_raw, second), (slots, page)])
    teacher(0)
    pl.semaphore_wait(barrier, rows_n - 1 + len(bits) + 1)
    t_start(0, (0,))
    teacher(1)
    t_start(0, (1, 2))

    values = student[...].astype(F32)
    inverse_norm = lax.rsqrt(jnp.sum(values * values, axis=1, keepdims=True) + 1e-06)
    unit = (values * inverse_norm).astype(BF16)
    s_row[block(c)] = unit
    s_col[block(a)] = unit

    steps = len(bits)
    p_start, p_pass, p_core, p_sent = plane(s_row, ds)
    p_start()
    for step in range(max(steps, rows_n - 1)):
        if step < rows_n - 1:
            for parts in ((0,), (1, 2)):
                t_recv(step, parts)
                if step + 1 < rows_n - 1:
                    t_start(step + 1, parts)
        if step < steps:
            p_pass(step)

    column = rows_n * r
    for b in range(rows_n):
        at = lax.broadcasted_iota(jnp.int32, (column, r), 0)
        places[:, b * r:(b + 1) * r] = (at == slots[b][0:1, :]).astype(F32).astype(BF16)
    piece = 512

    def own(n, carry):
        cut = block(n, piece)
        t_row[block(c), cut] = jnp.dot(
            places[block(a), :], t_raw[:, cut], preferred_element_type=F32).astype(BF16)
        return carry

    lax.fori_loop(0, dt // piece, own, 0)
    q_start, q_pass, q_core, q_sent = plane(t_row, dt)
    q_start()
    t_sent()
    s_start, s_recv, s_sent = line([(s_col, whole)])
    s_start(0)

    def every(n, carry):
        cut = block(n, piece)
        t_col[:, cut] = jnp.dot(places[...], t_raw[:, cut], preferred_element_type=F32).astype(BF16)
        return carry

    lax.fori_loop(0, dt // piece, every, 0)
    for step in range(max(steps, rows_n - 2)):
        if step < rows_n - 2:
            s_recv(step)
            s_start(step + 1)
        if step < steps:
            q_pass(step)
    p_core()
    q_core()
    q_sent()
    contract = (((1,), (1,)), ((), ()))

    def teacher_gram(i, carry):
        pair = block(i, 2 * r)
        differ[pair, :] = lax.dot_general(
            t_row[pair, :], t_col[...], contract, preferred_element_type=F32)
        return carry

    lax.fori_loop(0, chips, teacher_gram, 0)
    s_recv(rows_n - 2)

    loss_sum[...] = jnp.zeros_like(loss_sum)
    half = ds // 2
    core_base = take(chips)
    away_base = take(2 * chips)
    back = tuple(tuple(reversed(order)) for order in orders)

    def moved(index, mask):
        bit = 1
        while bit < chips:
            index = index + ((mask // bit) % 2) * bit * (1 - 2 * ((index // bit) % 2))
            bit *= 2
        return index

    def core_copy(turn):
        there = moved(chip, turn)
        return copy_to(
            t_row.at[block(there * 2 + 1 - core), 0:ds], t_raw.at[block(turn), 0:ds], core_base + turn, (a, flip(c, 1)))

    def away_copy(h, turn, bit):
        there = moved(chip, turn) * 2 + core
        return copy_to(
            t_row.at[block(there), h * half:(h + 1) * half], got.at[h * chips + turn],
            away_base + h * chips + turn, (a, flip(c, bit)))

    def tile(i, carry):
        turn = chips - 1 - i
        pair = block(moved(chip, turn), 2 * r)
        now = lax.dot_general(s_row[pair, :], s_col[...], contract, preferred_element_type=F32) - differ[pair, :]
        loss_sum[...] += jnp.sum(now * now, axis=0, keepdims=True)
        low = now.astype(BF16)
        for n in range(ds // piece):
            t_row[pair, n * piece:(n + 1) * piece] = jnp.dot(
                low, s_col[:, n * piece:(n + 1) * piece], preferred_element_type=F32).astype(BF16)
        core_copy(turn).start()

        @pl.when(i > 0)
        def _():
            last = turn + 1
            core_copy(last).wait_recv()
            mine = block(moved(chip, last) * 2 + core)
            t_row[mine, 0:ds] = (
                t_row[mine, 0:ds].astype(F32) + t_raw[block(last), 0:ds].astype(F32)).astype(BF16)
            for h in (0, 1):
                bit = back[h][0]

                @pl.when((last // (bit // 2)) % 2 == 1)
                def _():
                    away_copy(h, last, bit).start()

        return carry

    lax.fori_loop(0, chips, tile, 0)

    loss_z[a] = jnp.broadcast_to(jnp.sum(loss_sum[...], axis=1, keepdims=True), loss_z.shape[1:])
    loss_copies = []
    for k in range(1, rows_n):
        copy = copy_to(loss_z.at[a], loss_z.at[a], take(), ((a + k) % rows_n, c))
        copy.start()
        loss_copies.append(copy)

    core_copy(0).wait_recv()
    total[...] = t_row[block(c), 0:ds].astype(F32) + t_raw[block(0), 0:ds].astype(F32)
    left = [list(range(chips)) for _ in (0, 1)]
    away = []
    for step in range(steps):
        for h in (0, 1):
            bit = back[h][step]
            left[h] = [turn for turn in left[h] if not turn & (bit // 2)]
            for turn in left[h]:
                copy = away_copy(h, turn + bit // 2, bit)
                away.append(copy)
                copy.wait_recv()
                span = slice(h * half, (h + 1) * half)
                landed = got[h * chips + turn + bit // 2].astype(F32)
                if turn == 0:
                    total[:, span] += landed
                else:
                    mine = block(flip_all(c, 2 * turn))
                    t_row[mine, span] = (t_row[mine, span].astype(F32) + landed).astype(BF16)
                    if step + 1 < steps and turn & (back[h][step + 1] // 2):
                        away_copy(h, turn, back[h][step + 1]).start()

    for copy in loss_copies:
        copy.wait_recv()
    loss_now = loss_z[0]
    for b in range(1, rows_n):
        loss_now = loss_now + loss_z[b]
    sent = []
    for step in range(steps):
        loss_put[step] = loss_now
        copy = copy_to(loss_put.at[step], loss_got.at[step], take(), (a, flip(c, bits[step])))
        copy.start()
        copy.wait_recv()
        loss_now = loss_now + loss_got[step]
        sent.append(copy)
    loss_put[steps] = loss_now
    copy = copy_to(loss_put.at[steps], loss_got.at[steps], take(), (a, flip(c, 1)))
    copy.start()
    sent.append(copy)

    grad = total[...] * float(ds)
    values = student[...].astype(F32)
    inverse_norm = lax.rsqrt(jnp.sum(values * values, axis=1, keepdims=True) + 1e-06)
    unit = values * inverse_norm
    along = jnp.sum(unit * grad, axis=1, keepdims=True)
    grad_out[...] = inverse_norm * (grad - unit * along)

    copy.wait_recv()
    loss_out[...] = (loss_now + loss_got[steps]) * (ds / (total_rows * total_rows))

    for copy in sent + loss_copies + away:
        copy.wait_send()
    for i in range(chips):
        core_copy(i).wait_send()
    s_sent()
    p_sent()


def on_device(rows_n, cols_n, student, codes, scales, slot):
    r, ds = student.shape
    dt = codes.shape[1]
    total_rows = r * rows_n * cols_n
    chips = cols_n // 2
    steps = chips.bit_length() - 1
    count = 8 * (rows_n - 1) + 2 * (2 * (chips - 1) + 2 * chips)
    count += chips + 2 * chips + (rows_n - 1) + steps + 1
    vmem = pl.BlockSpec(memory_space=pltpu.VMEM)
    loss, grad = pl.pallas_call(
        functools.partial(kernel, rows_n, cols_n, total_rows),
        out_shape=(jax.ShapeDtypeStruct((8, 128), F32), jax.ShapeDtypeStruct((r, ds), F32)),
        in_specs=[vmem] * 4,
        out_specs=(vmem, vmem),
        scratch_shapes=[
            pltpu.VMEM((cols_n * r, ds), BF16),
            pltpu.VMEM((rows_n * r, ds), BF16),
            pltpu.VMEM((rows_n * r, dt), BF16),
            pltpu.VMEM((rows_n * r, dt), BF16),
            pltpu.VMEM((cols_n * r, dt), BF16),
            pltpu.VMEM((rows_n * r, rows_n * r), BF16),
            pltpu.VMEM((rows_n, 8, r), jnp.int32),
            pltpu.VMEM((cols_n * r, rows_n * r), F32),
            pltpu.VMEM((2 * chips, r, ds // 2), BF16),
            pltpu.VMEM((r, ds), F32),
            pltpu.VMEM((rows_n, 8, 128), F32),
            pltpu.VMEM((steps + 1, 8, 128), F32),
            pltpu.VMEM((steps + 1, 8, 128), F32),
            pltpu.VMEM((1, rows_n * r), F32),
            pltpu.SemaphoreType.DMA((count,)),
            pltpu.SemaphoreType.DMA((count,)),
        ],
        compiler_params=pltpu.CompilerParams(
            collective_id=0, has_side_effects=True, vmem_limit_bytes=62 * 1024 * 1024
        ),
    )(student, codes, scales, slot.reshape(1, r))
    return loss[0, 0], grad


def solution(mesh):
    rows_n, cols_n = mesh.shape["row"], mesh.shape["col"]
    return jax.shard_map(
        functools.partial(on_device, rows_n, cols_n),
        mesh=mesh,
        in_specs=(
            P(("row", "col"), None),
            P(("row", "col"), None),
            P(("row", "col"), None),
            P(("row", "col")),
        ),
        out_specs=(P(), P(("row", "col"), None)),
        check_vma=False,
    )
```

time: 147 us -> 145 us (0.986)
  Pallas kernels: 141 us -> 139 us
    pallas_call x1, Pallas kernels: 141 us -> 139 us  [on_device(): pl.pallas_call(functools.partial(kernel, rows_n, cols_n, total_rows), out...]
where the time goes in v2:
time: 145 us; the launch traced here: 144 us
  Pallas kernels  139 us (96%)
  local copies, waits for them, and re-layouts  4.9 us (3%)
    pallas_call x1, Pallas kernels, on_device(): pl.pallas_call(functools.partial(kernel, rows_n, cols_n, total_rows), out...  139 us
    unnamed x2, local copies, waits for them, and re-layouts  3.71 us

profile of v2, /device:TPU:0, one launch (start us, length us, event | category | flops | bytes accessed | tf_op | source)
XLA Modules:
  0.0 144.3 jit_solution(1198557083220139331)
XLA Ops:
  0.6 1.4 copy.6.scales
  2.0 138.7 %shard_map.59 = (f32[8,128]{1,0:T(8,128)}, f32[128,2048]{1,0:T(8,128)}) custom-call(bf16[128,2048]{1,0:T(8,128)(2,1)} %student.1, bf16[128,3584]{1,0:T(8,128)(2,1)} %codes.1, bf16[128,28]{1,0:T(8,128)(2,1)} %copy.6.scales, s32[1,128]{1,0:T(1,128)} %bitcast.2), custom_call_target="tpu_custom_call" | custom-call | tf_op jit(solution)/shard_map/pallas_call | solution.py:375
  140.8 1.2 slice.3
  142.0 2.3 %copy.8 = f32[128,2048]{1,0:T(8,128)} copy(f32[128,2048]{1,0:T(8,128)} %get-tuple-element.9) | data formatting | bytes 2097152

commit v3 on v2

--- a/solution.py
+++ b/solution.py
@@ -125,19 +125,19 @@
 
         return start, wait_recv, wait_send
 
-    def plane(ref, width):
+    def plane(ref, base, width):
         half = width // 2
         started = []
         hops, cores = {}, {}
 
         def hop(h, step, mask):
-            view = ref.at[block(flip_all(c, mask)), h * half:(h + 1) * half]
+            view = ref.at[block(flip_all(c, mask)), base + h * half:base + (h + 1) * half]
             hops[h, step, mask] = copy_to(view, view, take(), (a, flip(c, orders[h][step])))
             hops[h, step, mask].start()
             started.append(hops[h, step, mask])
 
         def to_core(h, mask):
-            view = ref.at[block(flip_all(c, mask)), h * half:(h + 1) * half]
+            view = ref.at[block(flip_all(c, mask)), base + h * half:base + (h + 1) * half]
             cores[h, mask] = copy_to(view, view, take(), (a, flip(c, 1)))
             cores[h, mask].start()
             started.append(cores[h, mask])
@@ -173,14 +173,16 @@
 
     whole = lambda ref, held: ref.at[block(held)]
     page = lambda ref, held: ref.at[held]
-    first = lambda ref, held: ref.at[block(2 * held, cut_rows)]
-    second = lambda ref, held: ref.at[block(2 * held + 1, cut_rows)]
-    t_start, t_recv, t_sent = line([(t_raw, first), (t_raw, second), (slots, page)])
+    wide = dt // 2
+    first = lambda ref, held: ref.at[block(2 * held, cut_rows), 0:wide]
+    second = lambda ref, held: ref.at[block(2 * held + 1, cut_rows), 0:wide]
+    third = lambda ref, held: ref.at[block(held), wide:dt]
+    t_start, t_recv, t_sent = line([(slots, page), (t_raw, first), (t_raw, second), (t_raw, third)])
     teacher(0)
     pl.semaphore_wait(barrier, rows_n - 1 + len(bits) + 1)
-    t_start(0, (0,))
+    t_start(0, (0, 1))
     teacher(1)
-    t_start(0, (1, 2))
+    t_start(0, (2,))
 
     values = student[...].astype(F32)
     inverse_norm = lax.rsqrt(jnp.sum(values * values, axis=1, keepdims=True) + 1e-06)
@@ -189,60 +191,81 @@
     s_col[block(a)] = unit
 
     steps = len(bits)
-    p_start, p_pass, p_core, p_sent = plane(s_row, ds)
+    p_start, p_pass, p_core, p_sent = plane(s_row, 0, ds)
     p_start()
     for step in range(max(steps, rows_n - 1)):
         if step < rows_n - 1:
-            for parts in ((0,), (1, 2)):
+            for parts in ((0, 1), (2,)):
                 t_recv(step, parts)
                 if step + 1 < rows_n - 1:
                     t_start(step + 1, parts)
         if step < steps:
             p_pass(step)
 
+    t_start(0, (3,))
+
     column = rows_n * r
     for b in range(rows_n):
         at = lax.broadcasted_iota(jnp.int32, (column, r), 0)
         places[:, b * r:(b + 1) * r] = (at == slots[b][0:1, :]).astype(F32).astype(BF16)
     piece = 512
+    narrow = 256
+    contract = (((1,), (1,)), ((), ()))
 
     def own(n, carry):
-        cut = block(n, piece)
+        cut = block(n, narrow)
         t_row[block(c), cut] = jnp.dot(
             places[block(a), :], t_raw[:, cut], preferred_element_type=F32).astype(BF16)
         return carry
 
-    lax.fori_loop(0, dt // piece, own, 0)
-    q_start, q_pass, q_core, q_sent = plane(t_row, dt)
+    def every(n, carry):
+        cut = block(n, narrow)
+        t_col[:, cut] = jnp.dot(places[...], t_raw[:, cut], preferred_element_type=F32).astype(BF16)
+        return carry
+
+    def teacher_gram(part):
+        def body(i, carry):
+            pair = block(i, 2 * r)
+            span = slice(part * wide, (part + 1) * wide)
+            gram = lax.dot_general(t_row[pair, span], t_col[:, span], contract, preferred_element_type=F32)
+            differ[pair, :] = differ[pair, :] + gram if part else gram
+            return carry
+
+        lax.fori_loop(0, chips, body, 0)
+
+    count = wide // narrow
+    lax.fori_loop(0, count, own, 0)
+    q_start, q_pass, q_core, q_sent = plane(t_row, 0, wide)
     q_start()
+    lax.fori_loop(0, count, every, 0)
+    for step in range(max(steps, rows_n - 2)):
+        if step < rows_n - 2:
+            t_recv(step, (3,))
+            t_start(step + 1, (3,))
+        if step < steps:
+            q_pass(step)
+    q_core()
+    teacher_gram(0)
+    t_recv(rows_n - 2, (3,))
+
+    lax.fori_loop(count, 2 * count, own, 0)
+    u_start, u_pass, u_core, u_sent = plane(t_row, wide, wide)
+    u_start()
     t_sent()
     s_start, s_recv, s_sent = line([(s_col, whole)])
     s_start(0)
-
-    def every(n, carry):
-        cut = block(n, piece)
-        t_col[:, cut] = jnp.dot(places[...], t_raw[:, cut], preferred_element_type=F32).astype(BF16)
-        return carry
-
-    lax.fori_loop(0, dt // piece, every, 0)
+    lax.fori_loop(count, 2 * count, every, 0)
     for step in range(max(steps, rows_n - 2)):
         if step < rows_n - 2:
             s_recv(step)
             s_start(step + 1)
         if step < steps:
-            q_pass(step)
+            u_pass(step)
     p_core()
-    q_core()
+    u_core()
+    teacher_gram(1)
     q_sent()
-    contract = (((1,), (1,)), ((), ()))
-
-    def teacher_gram(i, carry):
-        pair = block(i, 2 * r)
-        differ[pair, :] = lax.dot_general(
-            t_row[pair, :], t_col[...], contract, preferred_element_type=F32)
-        return carry
-
-    lax.fori_loop(0, chips, teacher_gram, 0)
+    u_sent()
     s_recv(rows_n - 2)
 
     loss_sum[...] = jnp.zeros_like(loss_sum)
@@ -307,9 +330,19 @@
 
     core_copy(0).wait_recv()
     total[...] = t_row[block(c), 0:ds].astype(F32) + t_raw[block(0), 0:ds].astype(F32)
+    for copy in loss_copies:
+        copy.wait_recv()
+    loss_now = loss_z[0]
+    for b in range(1, rows_n):
+        loss_now = loss_now + loss_z[b]
+    sent = []
     left = [list(range(chips)) for _ in (0, 1)]
     away = []
     for step in range(steps):
+        loss_put[step] = loss_now
+        hop = copy_to(loss_put.at[step], loss_got.at[step], take(), (a, flip(c, bits[step])))
+        hop.start()
+        sent.append(hop)
         for h in (0, 1):
             bit = back[h][step]
             left[h] = [turn for turn in left[h] if not turn & (bit // 2)]
@@ -326,20 +359,9 @@
                     t_row[mine, span] = (t_row[mine, span].astype(F32) + landed).astype(BF16)
                     if step + 1 < steps and turn & (back[h][step + 1] // 2):
                         away_copy(h, turn, back[h][step + 1]).start()
-
-    for copy in loss_copies:
-        copy.wait_recv()
-    loss_now = loss_z[0]
-    for b in range(1, rows_n):
-        loss_now = loss_now + loss_z[b]
-    sent = []
-    for step in range(steps):
-        loss_put[step] = loss_now
-        copy = copy_to(loss_put.at[step], loss_got.at[step], take(), (a, flip(c, bits[step])))
-        copy.start()
-        copy.wait_recv()
+        hop.wait_recv()
         loss_now = loss_now + loss_got[step]
-        sent.append(copy)
+
     loss_put[steps] = loss_now
     copy = copy_to(loss_put.at[steps], loss_got.at[steps], take(), (a, flip(c, 1)))
     copy.start()
@@ -369,7 +391,7 @@
     total_rows = r * rows_n * cols_n
     chips = cols_n // 2
     steps = chips.bit_length() - 1
-    count = 8 * (rows_n - 1) + 2 * (2 * (chips - 1) + 2 * chips)
+    count = 10 * (rows_n - 1) + 3 * (2 * (chips - 1) + 2 * chips)
     count += chips + 2 * chips + (rows_n - 1) + steps + 1
     vmem = pl.BlockSpec(memory_space=pltpu.VMEM)
     loss, grad = pl.pallas_call(

time: 145 us -> 135 us (0.931)
  Pallas kernels: 139 us -> 129 us
    pallas_call x1, Pallas kernels: 139 us -> 129 us  [on_device(): pl.pallas_call(functools.partial(kernel, rows_n, cols_n, total_rows), out...]
where the time goes in v3:
time: 135 us; the launch traced here: 134 us
  Pallas kernels  129 us (96%)
  local copies, waits for them, and re-layouts  4.9 us (4%)
    pallas_call x1, Pallas kernels, on_device(): pl.pallas_call(functools.partial(kernel, rows_n, cols_n, total_rows), out...  129 us
    unnamed x2, local copies, waits for them, and re-layouts  3.71 us

profile of v3, /device:TPU:0, one launch (start us, length us, event | category | flops | bytes accessed | tf_op | source)
XLA Modules:
  0.0 134.5 jit_solution(9130868273870247473)
XLA Ops:
  0.6 1.4 %copy.6.scales = bf16[128,28]{1,0:T(8,128)(2,1)} copy(bf16[128,28]{0,1:T(8,128)(2,1)} %param.6) | data formatting | bytes 14336 | tf_op args[2]
  2.0 129.0 %shard_map.59 = (f32[8,128]{1,0:T(8,128)}, f32[128,2048]{1,0:T(8,128)}) custom-call(bf16[128,2048]{1,0:T(8,128)(2,1)} %student.1, bf16[128,3584]{1,0:T(8,128)(2,1)} %codes.1, bf16[128,28]{1,0:T(8,128)(2,1)} %copy.6.scales, s32[1,128]{1,0:T(1,128)} %bitcast.2), custom_call_target="tpu_custom_call" | custom-call | tf_op jit(solution)/shard_map/pallas_call | solution.py:397
  131.0 1.2 slice.3
  132.2 2.3 %copy.8 = f32[128,2048]{1,0:T(8,128)} copy(f32[128,2048]{1,0:T(8,128)} %get-tuple-element.9) | data formatting | bytes 2097152

commit v4 on v3

--- a/solution.py
+++ b/solution.py
@@ -171,13 +171,16 @@
 
         return start, pass_on, wait_core, wait_send
 
-    whole = lambda ref, held: ref.at[block(held)]
     page = lambda ref, held: ref.at[held]
     wide = dt // 2
     first = lambda ref, held: ref.at[block(2 * held, cut_rows), 0:wide]
     second = lambda ref, held: ref.at[block(2 * held + 1, cut_rows), 0:wide]
-    third = lambda ref, held: ref.at[block(held), wide:dt]
-    t_start, t_recv, t_sent = line([(slots, page), (t_raw, first), (t_raw, second), (t_raw, third)])
+    third = lambda ref, held: ref.at[block(2 * held, cut_rows), wide:dt]
+    fourth = lambda ref, held: ref.at[block(2 * held + 1, cut_rows), wide:dt]
+    upper = lambda ref, held: ref.at[block(2 * held, cut_rows)]
+    lower = lambda ref, held: ref.at[block(2 * held + 1, cut_rows)]
+    t_start, t_recv, t_sent = line(
+        [(slots, page), (t_raw, first), (t_raw, second), (t_raw, third), (t_raw, fourth)])
     teacher(0)
     pl.semaphore_wait(barrier, rows_n - 1 + len(bits) + 1)
     t_start(0, (0, 1))
@@ -202,7 +205,7 @@
         if step < steps:
             p_pass(step)
 
-    t_start(0, (3,))
+    t_start(0, (3, 4))
 
     column = rows_n * r
     for b in range(rows_n):
@@ -240,25 +243,27 @@
     lax.fori_loop(0, count, every, 0)
     for step in range(max(steps, rows_n - 2)):
         if step < rows_n - 2:
-            t_recv(step, (3,))
-            t_start(step + 1, (3,))
+            for parts in ((3,), (4,)):
+                t_recv(step, parts)
+                t_start(step + 1, parts)
         if step < steps:
             q_pass(step)
     q_core()
     teacher_gram(0)
-    t_recv(rows_n - 2, (3,))
+    t_recv(rows_n - 2, (3, 4))
 
     lax.fori_loop(count, 2 * count, own, 0)
     u_start, u_pass, u_core, u_sent = plane(t_row, wide, wide)
     u_start()
     t_sent()
-    s_start, s_recv, s_sent = line([(s_col, whole)])
+    s_start, s_recv, s_sent = line([(s_col, upper), (s_col, lower)])
     s_start(0)
     lax.fori_loop(count, 2 * count, every, 0)
     for step in range(max(steps, rows_n - 2)):
         if step < rows_n - 2:
-            s_recv(step)
-            s_start(step + 1)
+            for parts in ((0,), (1,)):
+                s_recv(step, parts)
+                s_start(step + 1, parts)
         if step < steps:
             u_pass(step)
     p_core()
@@ -391,7 +396,7 @@
     total_rows = r * rows_n * cols_n
     chips = cols_n // 2
     steps = chips.bit_length() - 1
-    count = 10 * (rows_n - 1) + 3 * (2 * (chips - 1) + 2 * chips)
+    count = 14 * (rows_n - 1) + 3 * (2 * (chips - 1) + 2 * chips)
     count += chips + 2 * chips + (rows_n - 1) + steps + 1
     vmem = pl.BlockSpec(memory_space=pltpu.VMEM)
     loss, grad = pl.pallas_call(

time: 135 us -> 135 us (level)
  no operation moved by 1% of the time
where the time goes in v4:
time: 135 us
  Pallas kernels  129 us (96%)
  local copies, waits for them, and re-layouts  4.9 us (4%)
    pallas_call x1, Pallas kernels, on_device(): pl.pallas_call(functools.partial(kernel, rows_n, cols_n, total_rows), out...  129 us
    unnamed x2, local copies, waits for them, and re-layouts  3.71 us

profile of v4, /device:TPU:0, one launch (start us, length us, event | category | flops | bytes accessed | tf_op | source)
XLA Modules:
  0.0 134.7 jit_solution(14764497515980568642)
XLA Ops:
  0.6 1.4 %copy.6.scales = bf16[128,28]{1,0:T(8,128)(2,1)} copy(bf16[128,28]{0,1:T(8,128)(2,1)} %param.6) | data formatting | bytes 14336 | tf_op args[2]
  2.0 129.2 %shard_map.59 = (f32[8,128]{1,0:T(8,128)}, f32[128,2048]{1,0:T(8,128)}) custom-call(bf16[128,2048]{1,0:T(8,128)(2,1)} %student.1, bf16[128,3584]{1,0:T(8,128)(2,1)} %codes.1, bf16[128,28]{1,0:T(8,128)(2,1)} %copy.6.scales, s32[1,128]{1,0:T(1,128)} %bitcast.2), custom_call_target="tpu_custom_call" | custom-call | tf_op jit(solution)/shard_map/pallas_call | solution.py:402
  131.2 1.2 slice.3
  132.4 2.3 %copy.8 = f32[128,2048]{1,0:T(8,128)} copy(f32[128,2048]{1,0:T(8,128)} %get-tuple-element.9) | data formatting | bytes 2097152
